TPU v7x, 256 devices: a whole 4x4x8 slice. The times are simulated.
256 devices in a mesh: replica: 8 (over y, core), fsdp: 32 (over z, x).
Axes of the slice: x: 4, y: 4, z: 8, core: 2. Of those that a mesh axis runs over, the one named last changes fastest.
Arguments:
- local_params: float32 [8, 512, 14336], P('replica', 'fsdp'), may hold values from -6 to 6
- outer_base: float32 [512, 14336], P('fsdp'), may hold values from -6 to 6
- error_memory: float32 [8, 512, 14336], P('replica', 'fsdp'), may hold values from -4 to 4
- momentum: float32 [512, 14336], P('fsdp'), may hold values from -6 to 6
- start_seed: int32 [1], replicated, may hold values from 0 to 65520
Outputs:
- new_error: float32 [8, 512, 14336], P('replica', 'fsdp')
- new_base: float32 [512, 14336], P('fsdp')
- new_momentum: float32 [512, 14336], P('fsdp')
All inputs are finite; a program needn't handle non-finite values.
Results may differ from a plain program's by a relative error of at most 0.00007.
Values sent between devices are 32-bit elements; how exact they have to be, the bound alone decides.
A program may use at most 64 MiB of HBM per device.

v0:
```python
import jax
import jax.numpy as jnp
from jax import lax
from jax.sharding import PartitionSpec as P

RANK = 128


def start_factor(start_seed, col_count, rank_count):
    row_index = lax.broadcasted_iota(jnp.int32, (col_count, rank_count), 0)
    col_index = lax.broadcasted_iota(jnp.int32, (col_count, rank_count), 1)
    mixed = (181 * row_index + 359 * col_index + 1013 * start_seed[0]) % 65521
    hashed = (mixed * (mixed % 32749) + 7 * row_index + 3 * col_index) % 65521
    return (hashed.astype(jnp.float32) / 65521.0 - 0.5) * 3.4641016


def contract_rows(first, second):
    return lax.dot_general(first, second, (((0,), (0,)), ((), ())), precision=lax.Precision.HIGHEST)


def contract_cols(first, second):
    return lax.dot_general(first, second, (((1,), (1,)), ((), ())), precision=lax.Precision.HIGHEST)


def term_maker(corrected, ortho_mine):

    def right_term(column_start, column_count):
        return contract_rows(corrected, ortho_mine)

    return right_term


def on_device(local_params, outer_base, error_memory, momentum, start_seed):
    highest = lax.Precision.HIGHEST
    replicas = lax.axis_size("replica")
    col_count = outer_base.shape[1]
    block_cols = col_count // lax.axis_size(("replica", "fsdp"))
    starting = start_factor(start_seed, col_count, RANK)
    corrected = outer_base - local_params[0] + error_memory[0]
    left_terms = jnp.dot(corrected, starting, precision=highest)
    left_mine = lax.psum(left_terms, "replica") / replicas
    gram_matrix = lax.psum(contract_rows(left_mine, left_mine), "fsdp")
    chol_factor = jnp.linalg.cholesky(gram_matrix)
    ortho_mine = jax.scipy.linalg.solve_triangular(chol_factor, left_mine.T, lower=True).T
    right_term = term_maker(corrected, ortho_mine)
    right_mine = (
        lax.psum_scatter(
            right_term(jnp.int32(0), block_cols * lax.axis_size(("replica", "fsdp"))),
            ("replica", "fsdp"),
            scatter_dimension=0,
            tiled=True,
        )
        / replicas
    )
    approx = contract_cols(
        ortho_mine, lax.all_gather(right_mine, ("replica", "fsdp"), axis=0, tiled=True)
    )
    new_error = (corrected - approx)[None]
    new_momentum = 0.9 * momentum + approx
    new_base = outer_base - 0.7 * (approx + 0.9 * new_momentum)
    return (new_error, new_base, new_momentum)


def solution(mesh):
    placed = (
        P("replica", "fsdp", None),
        P("fsdp", None),
        P("replica", "fsdp", None),
        P("fsdp", None),
        P(),
    )
    return jax.shard_map(
        on_device,
        mesh=mesh,
        in_specs=placed,
        out_specs=(P("replica", "fsdp", None), P("fsdp", None), P("fsdp", None)),
        check_vma=False,
    )
```

profile of v0, /device:TPU:1, one launch (start us, length us, event | category | flops | bytes accessed | tf_op | source)
XLA Modules:
  0.0 1636.3 jit_solution(706681151045573666)
XLA Ops:
  7.2 0.0 all-reduce.3.cloned.1.call-start
  7.9 1.9 bitcast_add_fusion
  9.7 19.1 %fusion.8 = f32[16,128]{1,0:T(8,128)S(1)} fusion(f32[16,14336]{1,0:T(8,128)S(1)} %bitcast_add_fusion, s32[128]{0:T(128)S(1)} %get-tuple-element.8, s32[14336]{0:T(1024)S(1)} %get-tuple-element.6, s32[]{:T(128)} %bitcast.2, s32[128]{0:T(128)S(1)} %get-tuple-element.9, s32[14336]{0:T(1024)S(1)} %get-tuple-element.7), kind=kOutput, calls=%fused_computation.11 | convolution fusion | flops 401866752 | bytes 1041412 | tf_op jit(solution)/shard_map/dot_general | solution.py:40
  28.9 15.2 psum.14
  44.1 0.9 fusion.37
  45.1 0.0 all-reduce.3.cloned.1.call-update
  45.1 0.0 reduce-scatter.5.cloned.1.call-start
  45.1 136.1 %all-reduce.3.cloned.1.call-done = f32[128,128]{0,1:T(8,128)} async-done(((f32[128,128]{0,1:T(8,128)}), f32[128,128]{0,1:T(8,128)}) %all-reduce.3.cloned.1.call-update) | async-done | bytes 65552 | tf_op jit(solution)/shard_map/psum | solution.py:42
  181.3 0.9 copy.11
  182.2 0.9 fusion.35
  183.0 11.7 cholesky.16
  194.8 0.6 compare_reduce_fusion
  195.4 0.7 fusion.32
  196.1 9.8 custom-call.7
  205.9 0.2 fusion.33
  206.1 13.7 fusion.49
  219.8 0.0 copy-start
  219.8 0.0 copy-start.1
  219.8 0.0 reduce-scatter.5.cloned.1.call-update
  219.8 0.0 all-gather.2.cloned.1.call-start
  219.9 1223.3 %reduce-scatter.5.cloned.1.call-done = f32[56,128]{1,0:T(8,128)} async-done(((f32[14336,128]{1,0:T(8,128)}), f32[56,128]{1,0:T(8,128)}) %reduce-scatter.5.cloned.1.call-update) | async-done | bytes 28688
  1443.2 1.4 broadcast_multiply_fusion
  1444.5 0.0 all-gather.2.cloned.1.call-update
  1444.5 175.9 %all-gather.2.cloned.1.call-done = f32[14336,128]{1,0:T(8,128)} async-done(((f32[56,128]{1,0:T(8,128)}), f32[14336,128]{1,0:T(8,128)}) %all-gather.2.cloned.1.call-update) | async-done | bytes 7340048 | tf_op jit(solution)/shard_map/all_gather | solution.py:56
  1620.4 0.0 copy-done
  1620.4 0.0 copy-done.1
  1620.4 9.4 multiply_subtract_fusion
  (3 shorter events, 0.1 us)
Async XLA Ops:
  7.2 174.1 %all-reduce.3.cloned.1.call-start = ((), (), s32[]{:S(2)}) async-start(), calls=%async_computation.1 | async-start | bytes 131072 | tf_op jit(solution)/shard_map/psum | solution.py:42
  45.1 1398.1 %reduce-scatter.5.cloned.1.call-start = ((), (), s32[]{:S(2)}) async-start(), calls=%async_computation.3 | async-start | bytes 7368704
  219.8 1400.6 %copy-start = (f32[16,14336]{1,0:T(8,128)S(1)}, f32[16,14336]{1,0:T(8,128)}, u32[]{:S(2)}) copy-start(f32[16,14336]{1,0:T(8,128)} %param.6) | copy-start | bytes 2752516
  219.8 1400.6 %copy-start.1 = (f32[16,14336]{1,0:T(8,128)S(1)}, f32[16,14336]{1,0:T(8,128)}, u32[]{:S(2)}) copy-start(f32[16,14336]{1,0:T(8,128)} %param.8) | copy-start | bytes 2752516
  219.8 1400.6 %all-gather.2.cloned.1.call-start = ((), (), s32[]{:S(2)}) async-start(), calls=%async_computation.2 | async-start | bytes 7368704 | tf_op jit(solution)/shard_map/all_gather | solution.py:56
Sparse Core Ops, SparseCore 0:
  45.2 136.0 all-reduce.2
  220.0 1223.1 reduce-scatter.4
  1447.9 172.4 all-gather.1
where the time goes:
time: 1640 us
  waiting for transfers between devices  1540 us (94%)
  matrix products  43.3 us (3%)
  other arithmetic  26.9 us (2%)
    unnamed x4, waiting for transfers between devices  1220 us
    all_gather x1, waiting for transfers between devices, on_device(): lax.all_gather(right_mine, ('replica', 'fsdp'), axis=0, tiled=True)  176 us
    psum x1, waiting for transfers between devices, on_device(): gram_matrix = lax.psum(contract_rows(left_mine, left_mine), 'fsdp')  136 us
  transfers between devices with their start and end apart: 3, of which 3 were waited for; matrix products, arithmetic and copies ran while one was open for 0% of the time, Pallas kernels for 0%

commit v1 on v0

v1 whole, which is shorter than its diff:
```python
import functools

import jax
import jax.numpy as jnp
from jax import lax
from jax.experimental import pallas as pl
from jax.experimental.pallas import tpu as pltpu
from jax.sharding import PartitionSpec as P

RANK = 128
LANES = 128
SUBS = 8
HIGHEST = lax.Precision.HIGHEST
MESH = pl.DeviceIdType.MESH


def owner_of(tile, tiles, fsdp):
    return tile if tiles == fsdp else tile + 1 + tile // 8


def tile_of(f, tiles, fsdp):
    if tiles == fsdp:
        return f >= 0, f
    tile = f - 1 - f // 9
    return jnp.logical_and(lax.rem(f, 9) != 0, tile < tiles), tile


def write_start_factor(seed, first_row, out_ref):
    k = lax.broadcasted_iota(jnp.int32, (SUBS, LANES), 1)
    j = lax.broadcasted_iota(jnp.int32, (SUBS, LANES), 0) + first_row
    mixed = lax.rem(181 * j + 359 * k + 1013 * seed, 65521)
    added = 7 * j + 3 * k

    def rows(i, carry):
        mixed, added = carry
        low = jnp.where(mixed >= 65498, mixed - 65498, jnp.where(mixed >= 32749, mixed - 32749, mixed))
        value = mixed * low + added
        quotient = (value.astype(jnp.float32) * (1.0 / 65521.0)).astype(jnp.int32)
        rest = value - quotient * 65521
        rest = jnp.where(rest < 0, rest + 65521, rest)
        rest = jnp.where(rest >= 65521, rest - 65521, rest)
        drawn = (rest.astype(jnp.float32) * (1.0 / 65521.0) - 0.5) * 3.4641016
        out_ref[pl.ds(pl.multiple_of(i * SUBS, SUBS), SUBS), :] = drawn
        mixed = mixed + 181 * SUBS
        return jnp.where(mixed >= 65521, mixed - 65521, mixed), added + 7 * SUBS

    lax.fori_loop(0, out_ref.shape[0] // SUBS, rows, (mixed, added), unroll=8)


def solve(mg, mw):
    sub = lax.broadcasted_iota(jnp.int32, (SUBS, LANES), 0)

    def col(x, lane):
        return jnp.broadcast_to(x[:, lane : lane + 1], (SUBS, LANES))

    def row(x, i):
        return jnp.broadcast_to(x[i : i + 1, :], (SUBS, LANES))

    panels = RANK // SUBS
    for p in range(panels):
        pg, pw = mg[p], mw[p]
        cols = [col(pg, SUBS * p + j) for j in range(SUBS)]
        for i in range(SUBS):
            scale = 1.0 / row(cols[i], i)
            here = sub == i
            by = cols[i]

            def step(x):
                pivot_row = row(x, i) * scale
                return jnp.where(here, pivot_row, x - by * pivot_row)

            pg, pw = step(pg), step(pw)
            for j in range(i + 1, SUBS):
                cols[j] = step(cols[j])
        g_rows = [row(pg, j) for j in range(SUBS)]
        w_rows = [row(pw, j) for j in range(SUBS)]
        for q in [(p + 1 + k) % panels for k in range(panels - 1)]:
            a, b = mg[q], mw[q]
            by = [col(a, SUBS * p + j) for j in range(SUBS)]

            def taken(rows):
                t = [by[j] * rows[j] for j in range(SUBS)]
                return ((t[0] + t[1]) + (t[2] + t[3])) + ((t[4] + t[5]) + (t[6] + t[7]))

            if p < panels - 1:
                mg[q] = a - taken(g_rows)
            mw[q] = b - taken(w_rows)
        if p < panels - 1:
            mg[p] = pg
        mw[p] = pw


def wait_for(ref, sem):
    pltpu.make_async_copy(ref, ref, sem).wait()


def kernel(
    replicas, fsdp, tiles,
    seed_ref, lp_hbm, base_hbm, err_hbm, out_hbm,
    cor, basev, errv, sib, rs, blk, start, parts, left, at, ap, apx, mg, mw,
    load_sem, p1_send, p1_recv, p2_send, p2_recv, p3_sem, p4_sem, px_sem, p5_sem, p7_sem,
    p8_send, p8_recv, p9_send, p9_recv, out_sem,
):
    chips = replicas // 2
    width = tiles * LANES
    r = lax.axis_index("replica")
    f = lax.axis_index("fsdp")
    c = lax.rem(r, 2)
    y = r // 2
    sibling = {"replica": 2 * y + 1 - c, "fsdp": f}
    shifts = [1, 3, 2, 0] if chips == 4 else [*range(1, chips), 0]

    def cols(block):
        return pl.ds(pl.multiple_of(block * width, LANES), width)

    def chip(shift):
        return lax.rem(y + shift, chips)

    def send(src, dst, s, d, to):
        pltpu.make_async_remote_copy(
            src_ref=src, dst_ref=dst, send_sem=s, recv_sem=d, device_id=to, device_id_type=MESH
        ).start()

    order = [2 * chip(s) + 1 - c for s in shifts] + [2 * chip(s) + c for s in shifts]
    loads = []
    for n, block in enumerate(order):
        at_cols = cols(block)
        three = [
            pltpu.make_async_copy(src.at[:, :, at_cols], dst.at[:, :, at_cols], load_sem.at[n, i])
            for i, (src, dst) in enumerate(((lp_hbm, cor), (base_hbm, basev), (err_hbm, errv)))
        ]
        for copy in three:
            copy.start()
        loads.append(three)

    barrier = pltpu.get_barrier_semaphore()
    for k in range(1, replicas):
        pl.semaphore_signal(
            barrier, inc=1, device_id={"replica": lax.rem(r + k, replicas), "fsdp": f}, device_id_type=MESH
        )

    def greet(k, _):
        pl.semaphore_signal(
            barrier, inc=1, device_id={"replica": r, "fsdp": lax.rem(f + k, fsdp)}, device_id_type=MESH
        )
        return 0

    lax.fori_loop(1, fsdp, greet, 0)

    write_start_factor(seed_ref[0], r * width, start)

    def correct(n):
        for copy in loads[n]:
            copy.wait()
        at_cols = cols(order[n])
        cor[:, :, at_cols] = basev[:, :, at_cols] - cor[:, :, at_cols] + errv[:, :, at_cols]

    correct(0)
    pl.semaphore_wait(barrier, replicas - 1 + fsdp - 1)

    for k in range(chips):
        if k > 0:
            correct(k)
        send(cor.at[:, :, cols(order[k])], sib.at[k], p1_send.at[k], p1_recv.at[k], sibling)
    for k, shift in enumerate(shifts):
        correct(chips + k)
        wait_for(sib.at[k], p1_recv.at[k])
        sib[k] = sib[k] + cor[:, :, cols(order[chips + k])]
        if shift:
            send(sib.at[k], rs.at[k], p2_send.at[k], p2_recv.at[k], {"replica": 2 * chip(shift) + c, "fsdp": f})
    total = sib[chips - 1]
    for k in range(chips - 1):
        wait_for(rs.at[k], p2_recv.at[k])
        total = total + rs[k]
    blk[...] = total * (1.0 / replicas)

    rows = 2 * blk.shape[1]
    parts[r] = jnp.dot(
        blk[...].reshape(rows, width), start[...], precision=HIGHEST, preferred_element_type=jnp.float32
    ).reshape(parts.shape[1:])
    for k in range(1, replicas):
        send(parts.at[r], parts.at[r], p3_sem.at[0], p3_sem.at[1], {"replica": lax.rem(r + k, replicas), "fsdp": f})

    has_tile, my_tile = tile_of(f, 2 * tiles, fsdp)
    owner = jnp.logical_and(has_tile, lax.rem(my_tile, 2) == c)
    my_tile = my_tile // 2
    for t in range(tiles):
        to = owner_of(2 * t + c, 2 * tiles, fsdp)
        tile = blk.at[:, :, t * LANES : (t + 1) * LANES]

        @pl.when(to != f)
        def _():
            send(tile, at.at[:, f], p5_sem.at[0], p5_sem.at[1], {"replica": r, "fsdp": to})

        @pl.when(to == f)
        def _():
            at[:, f] = tile[...]

    wait_for(parts.at[pl.ds(0, replicas - 1)], p3_sem.at[1])
    mine = parts[0, c]
    for k in range(1, replicas):
        mine = mine + parts[k, c]
    left[c, f] = mine

    def spread(k, _):
        send(left.at[c, f], left.at[c, f], p4_sem.at[0], p4_sem.at[1], {"replica": r, "fsdp": lax.rem(f + k, fsdp)})
        return 0

    lax.fori_loop(1, fsdp, spread, 0)
    wait_for(left.at[c, pl.ds(0, fsdp - 1)], p4_sem.at[1])
    send(left.at[c], left.at[c], px_sem.at[0], px_sem.at[1], sibling)
    wait_for(left.at[1 - c], px_sem.at[1])

    my_cols = pl.ds(pl.multiple_of((r * tiles + my_tile) * LANES, LANES), LANES)

    @pl.when(owner)
    def _():
        wait_for(at.at[:, pl.ds(0, fsdp - 1)], p5_sem.at[1])
        whole = left[...].reshape(fsdp * rows, RANK)
        against = (((0,), (0,)), ((), ()))
        mg[...] = lax.dot_general(
            whole, whole, against, precision=HIGHEST, preferred_element_type=jnp.float32
        ).reshape(mg.shape)
        mw[...] = lax.dot_general(
            whole, at[...].reshape(fsdp * rows, LANES), against, precision=HIGHEST, preferred_element_type=jnp.float32
        ).reshape(mw.shape)
        solve(mg, mw)
        ap[...] = jnp.dot(
            whole, mw[...].reshape(RANK, LANES), precision=HIGHEST, preferred_element_type=jnp.float32
        ).reshape(ap.shape)

        def give(k, _):
            to = lax.rem(f + k, fsdp)
            send(ap.at[:, to], apx.at[:, :, my_cols], p7_sem.at[0], p7_sem.at[1], {"replica": r, "fsdp": to})
            return 0

        lax.fori_loop(1, fsdp, give, 0)
        apx[:, :, my_cols] = ap[:, f]
        wait_for(at.at[:, pl.ds(0, tiles - 1)], p7_sem.at[1])

    @pl.when(jnp.logical_not(owner))
    def _():
        wait_for(at.at[:, pl.ds(0, tiles)], p7_sem.at[1])

    def place(block):
        return apx.at[:, :, cols(block)]

    for k, shift in enumerate(shifts[:-1]):
        send(place(r), place(r), p8_send.at[k], p8_recv.at[k], {"replica": 2 * chip(shift) + c, "fsdp": f})
    send(place(r), place(r), p9_send.at[chips - 1], p9_recv.at[chips - 1], sibling)
    outs = []

    def write_out(block):
        copy = pltpu.make_async_copy(place(block), out_hbm.at[:, :, cols(block)], out_sem.at[len(outs)])
        copy.start()
        outs.append(copy)

    write_out(r)
    for k, shift in enumerate(shifts[:-1]):
        block = 2 * chip(chips - shift) + c
        wait_for(place(block), p8_recv.at[k])
        send(place(block), place(block), p9_send.at[k], p9_recv.at[k], sibling)
        write_out(block)
    for k, shift in [(chips - 1, 0), *enumerate(shifts[:-1])]:
        block = 2 * chip(chips - shift) + 1 - c
        wait_for(place(block), p9_recv.at[k])
        write_out(block)

    for k in range(chips):
        wait_for(sib.at[k], p1_send.at[k])
        wait_for(sib.at[k], p9_send.at[k])
        if k < chips - 1:
            wait_for(sib.at[k], p2_send.at[k])
            wait_for(sib.at[k], p8_send.at[k])
    wait_for(parts.at[pl.ds(0, replicas - 1)], p3_sem.at[0])
    wait_for(left.at[c, pl.ds(0, fsdp - 1)], p4_sem.at[0])
    wait_for(left.at[c], px_sem.at[0])

    own_tile_here = jnp.logical_and(owner, my_tile < tiles)

    @pl.when(own_tile_here)
    def _():
        wait_for(at.at[:, pl.ds(0, tiles - 1)], p5_sem.at[0])
        wait_for(ap.at[:, pl.ds(0, fsdp - 1)], p7_sem.at[0])

    @pl.when(jnp.logical_not(own_tile_here))
    def _():
        wait_for(at.at[:, pl.ds(0, tiles)], p5_sem.at[0])

    for copy in outs:
        copy.wait()


def approximate(local_params, outer_base, error_memory, start_seed):
    replicas, fsdp = lax.axis_size("replica"), lax.axis_size("fsdp")
    rows, columns = outer_base.shape
    half = rows // 2
    tiles = columns // replicas // LANES
    width = tiles * LANES
    chips = replicas // 2
    f32 = jnp.float32
    whole = (2, half, columns)
    dma = pltpu.SemaphoreType.DMA
    anywhere = pl.BlockSpec(memory_space=pl.ANY)
    found = pl.pallas_call(
        functools.partial(kernel, replicas, fsdp, tiles),
        out_shape=jax.ShapeDtypeStruct(whole, f32),
        in_specs=[pl.BlockSpec(memory_space=pltpu.SMEM), anywhere, anywhere, anywhere],
        out_specs=anywhere,
        scratch_shapes=[
            pltpu.VMEM(whole, f32),
            pltpu.VMEM(whole, f32),
            pltpu.VMEM(whole, f32),
            pltpu.VMEM((chips, 2, half, width), f32),
            pltpu.VMEM((chips - 1, 2, half, width), f32),
            pltpu.VMEM((2, half, width), f32),
            pltpu.VMEM((width, RANK), f32),
            pltpu.VMEM((replicas, 2, half, RANK), f32),
            pltpu.VMEM((2, fsdp, half, RANK), f32),
            pltpu.VMEM((2, fsdp, half, LANES), f32),
            pltpu.VMEM((2, fsdp, half, LANES), f32),
            pltpu.VMEM(whole, f32),
            pltpu.VMEM((RANK // SUBS, SUBS, RANK), f32),
            pltpu.VMEM((RANK // SUBS, SUBS, LANES), f32),
            dma((replicas, 3)),
            dma((chips,)),
            dma((chips,)),
            dma((chips,)),
            dma((chips,)),
            dma((2,)),
            dma((2,)),
            dma((2,)),
            dma((2,)),
            dma((2,)),
            dma((chips,)),
            dma((chips,)),
            dma((chips,)),
            dma((chips,)),
            dma((replicas,)),
        ],
        compiler_params=pltpu.CompilerParams(
            collective_id=0, has_side_effects=True, vmem_limit_bytes=48 * 1024 * 1024
        ),
        cost_estimate=pl.CostEstimate(flops=10**9, bytes_accessed=4 * 10**6, transcendentals=0),
        name="approximate",
    )(
        start_seed,
        local_params.reshape(whole),
        outer_base.reshape(whole),
        error_memory.reshape(whole),
    )
    return found.reshape(rows, columns)


def on_device(local_params, outer_base, error_memory, momentum, start_seed):
    approx = approximate(local_params[0], outer_base, error_memory[0], start_seed)
    corrected = outer_base - local_params[0] + error_memory[0]
    new_error = (corrected - approx)[None]
    new_momentum = 0.9 * momentum + approx
    new_base = outer_base - 0.7 * (approx + 0.9 * new_momentum)
    return (new_error, new_base, new_momentum)


def solution(mesh):
    placed = (
        P("replica", "fsdp", None),
        P("fsdp", None),
        P("replica", "fsdp", None),
        P("fsdp", None),
        P(),
    )
    return jax.shard_map(
        on_device,
        mesh=mesh,
        in_specs=placed,
        out_specs=(P("replica", "fsdp", None), P("fsdp", None), P("fsdp", None)),
        check_vma=False,
    )
```

time: 1640 us -> 62.2 us (0.04)
  waiting for transfers between devices: 1540 us -> 0 us
  Pallas kernels: 0 us -> 55.4 us
  matrix products: 43.3 us -> 0 us
  other arithmetic: 26.9 us -> 1.75 us
    unnamed x4 -> x0, waiting for transfers between devices: 1220 us -> none
    all_gather x1 -> x0, waiting for transfers between devices: 176 us -> none  [on_device(): lax.all_gather(right_mine, ('replica', 'fsdp'), axis=0, tiled=True)]
    psum x1 -> x0, waiting for transfers between devices: 136 us -> none  [on_device(): gram_matrix = lax.psum(contract_rows(left_mine, left_mine), 'fsdp')]
    pallas_call x0 -> x1, Pallas kernels: none -> 55.4 us  [approximate(): pl.pallas_call(functools.partial(kernel, replicas, fsdp, tiles), out_shap...]
    dot_general x4 -> x0, matrix products: 43.2 us -> none  [the longest x1 19.1 us: on_device(): left_terms = jnp.dot(corrected, starting, precision=highest)]
    another operation x5 -> x0, other arithmetic: 22.9 us -> none  [the longest x3 12.4 us: on_device(): chol_factor = jnp.linalg.cholesky(gram_matrix)]
  transfers between devices with their start and end apart: 3 -> 0, of which waited for: 3 -> 0; matrix products, arithmetic and copies ran while one was open for 0% -> 0% of each run, Pallas kernels for 0% -> 0%
where the time goes in v1:
time: 62.2 us; the launch traced here: 62 us
  Pallas kernels  55.4 us (89%)
  local copies, waits for them, and re-layouts  3.53 us (6%)
  other arithmetic  1.75 us (3%)
  between operations  1.3 us (2%)
    pallas_call x1, Pallas kernels, approximate(): pl.pallas_call(functools.partial(kernel, replicas, fsdp, tiles), out_shap...  55.4 us
    unnamed x8, local copies, waits for them, and re-layouts  3.53 us
    sub x1, other arithmetic, on_device(): new_base = outer_base - 0.7 * (approx + 0.9 * new_momentum)  1.75 us

profile of v1, /device:TPU:1, one launch (start us, length us, event | category | flops | bytes accessed | tf_op | source)
XLA Modules:
  0.0 62.0 jit_solution(14882365916859474903)
XLA Ops:
  1.3 0.0 copy-start
  1.3 1.2 %copy-done = f32[16,14336]{1,0:T(8,128)S(1)} copy-done((f32[16,14336]{1,0:T(8,128)S(1)}, f32[16,14336]{1,0:T(8,128)}, u32[]{:S(2)}) %copy-start) | copy-done | bytes 917528
  2.5 0.0 copy-start.1
  2.5 1.2 %copy-done.1 = f32[1,16,14336]{2,1,0:T(8,128)S(1)} copy-done((f32[1,16,14336]{2,1,0:T(8,128)S(1)}, f32[1,16,14336]{2,1,0:T(8,128)}, u32[]{:S(2)}) %copy-start.1) | copy-done | bytes 917528
  3.6 0.0 copy-start.2
  3.6 1.2 %copy-done.2 = f32[1,16,14336]{2,1,0:T(8,128)S(1)} copy-done((f32[1,16,14336]{2,1,0:T(8,128)S(1)}, f32[1,16,14336]{2,1,0:T(8,128)}, u32[]{:S(2)}) %copy-start.2) | copy-done | bytes 917528
  4.8 0.0 copy-start.3
  4.8 55.4 %approximate.1 = f32[2,8,14336]{2,1,0:T(8,128)S(1)} custom-call(s32[1]{0:T(128)S(6)} %copy.8.seed_ref, f32[2,8,14336]{2,1,0:T(8,128)S(1)} %bitcast.25, f32[2,8,14336]{2,1,0:T(8,128)S(1)} %bitcast.24, f32[2,8,14336]{2,1,0:T(8,128)S(1)} %bitcast.26), custom_call_target="tpu_custom_call" | custom-call | flops 1000000000 | bytes 4000000 | tf_op jit(solution)/shard_map/approximate/pallas_call | solution.py:305
  60.2 0.0 copy-done.3
  60.2 1.8 %fusion.2 = (f32[16,14336]{1,0:T(8,128)}, f32[16,14336]{1,0:T(8,128)}, f32[1,16,14336]{2,1,0:T(8,128)}) fusion(f32[16,14336]{1,0:T(8,128)S(1)} %copy-done, f32[2,8,14336]{2,1,0:T(8,128)S(1)} %approximate.1, f32[16,14336]{1,0:T(8,128)S(1)} %copy-done.3, f32[1,16,14336]{2,1,0:T(8,128)S(1)} %copy-done.2, f32[1,16,14336]{2,1,0:T(8,128)S(1)} %copy-done.1), kind=kLoop, calls=%fused_computation.5 | loop fusion | flops 2064384 | bytes 7340032 | tf_op jit(solution)/shard_map/sub | solution.py:360
Async XLA Ops:
  1.3 1.2 %copy-start = (f32[16,14336]{1,0:T(8,128)S(1)}, f32[16,14336]{1,0:T(8,128)}, u32[]{:S(2)}) copy-start(f32[16,14336]{1,0:T(8,128)} %param.6) | copy-start | bytes 2752516
  2.5 1.2 %copy-start.1 = (f32[1,16,14336]{2,1,0:T(8,128)S(1)}, f32[1,16,14336]{2,1,0:T(8,128)}, u32[]{:S(2)}) copy-start(f32[1,16,14336]{2,1,0:T(8,128)} %param.5) | copy-start | bytes 2752516
  3.6 1.2 %copy-start.2 = (f32[1,16,14336]{2,1,0:T(8,128)S(1)}, f32[1,16,14336]{2,1,0:T(8,128)}, u32[]{:S(2)}) copy-start(f32[1,16,14336]{2,1,0:T(8,128)} %param.7) | copy-start | bytes 2752516
  4.8 55.4 %copy-start.3 = (f32[16,14336]{1,0:T(8,128)S(1)}, f32[16,14336]{1,0:T(8,128)}, u32[]{:S(2)}) copy-start(f32[16,14336]{1,0:T(8,128)} %param.8) | copy-start | bytes 2752516

commit v2 on v1

v2 whole, which is shorter than its diff:
```python
import functools

import jax
import jax.numpy as jnp
from jax import lax
from jax.experimental import pallas as pl
from jax.experimental.pallas import tpu as pltpu
from jax.sharding import PartitionSpec as P

RANK = 128
LANES = 128
SUBS = 8
HIGHEST = lax.Precision.HIGHEST
MESH = pl.DeviceIdType.MESH


def owner_of(tile, tiles, fsdp):
    return tile if tiles == fsdp else tile + 1 + tile // 8


def tile_of(f, tiles, fsdp):
    if tiles == fsdp:
        return f >= 0, f
    tile = f - 1 - f // 9
    return jnp.logical_and(lax.rem(f, 9) != 0, tile < tiles), tile


def write_start_factor(seed, first_row, out_ref):
    k = lax.broadcasted_iota(jnp.int32, (SUBS, LANES), 1)
    j = lax.broadcasted_iota(jnp.int32, (SUBS, LANES), 0) + first_row
    mixed = lax.rem(181 * j + 359 * k + 1013 * seed, 65521)
    added = 7 * j + 3 * k

    def rows(i, carry):
        mixed, added = carry
        low = jnp.where(mixed >= 65498, mixed - 65498, jnp.where(mixed >= 32749, mixed - 32749, mixed))
        value = mixed * low + added
        quotient = (value.astype(jnp.float32) * (1.0 / 65521.0)).astype(jnp.int32)
        rest = value - quotient * 65521
        rest = jnp.where(rest < 0, rest + 65521, rest)
        rest = jnp.where(rest >= 65521, rest - 65521, rest)
        drawn = (rest.astype(jnp.float32) * (1.0 / 65521.0) - 0.5) * 3.4641016
        out_ref[pl.ds(pl.multiple_of(i * SUBS, SUBS), SUBS), :] = drawn
        mixed = mixed + 181 * SUBS
        return jnp.where(mixed >= 65521, mixed - 65521, mixed), added + 7 * SUBS

    lax.fori_loop(0, out_ref.shape[0] // SUBS, rows, (mixed, added), unroll=8)


def solve(mg, mw):
    sub = lax.broadcasted_iota(jnp.int32, (SUBS, LANES), 0)

    def col(x, lane):
        return jnp.broadcast_to(x[:, lane : lane + 1], (SUBS, LANES))

    def row(x, i):
        return jnp.broadcast_to(x[i : i + 1, :], (SUBS, LANES))

    panels = RANK // SUBS
    for p in range(panels):
        pg, pw = mg[p], mw[p]
        cols = [col(pg, SUBS * p + j) for j in range(SUBS)]
        for i in range(SUBS):
            scale = 1.0 / row(cols[i], i)
            here = sub == i
            by = cols[i]

            def step(x):
                pivot_row = row(x, i) * scale
                return jnp.where(here, pivot_row, x - by * pivot_row)

            pg, pw = step(pg), step(pw)
            for j in range(i + 1, SUBS):
                cols[j] = step(cols[j])
        g_rows = [row(pg, j) for j in range(SUBS)]
        w_rows = [row(pw, j) for j in range(SUBS)]
        for q in [(p + 1 + k) % panels for k in range(panels - 1)]:
            a, b = mg[q], mw[q]
            by = [col(a, SUBS * p + j) for j in range(SUBS)]

            def taken(rows):
                t = [by[j] * rows[j] for j in range(SUBS)]
                return ((t[0] + t[1]) + (t[2] + t[3])) + ((t[4] + t[5]) + (t[6] + t[7]))

            if p < panels - 1:
                mg[q] = a - taken(g_rows)
            mw[q] = b - taken(w_rows)
        if p < panels - 1:
            mg[p] = pg
        mw[p] = pw


def wait_for(ref, sem):
    if 0 in ref.shape:
        return
    pltpu.make_async_copy(ref, ref, sem).wait()


def kernel(
    replicas, fsdp, tiles,
    seed_ref, lp_hbm, base_hbm, err_hbm, apx, cor, basev,
    errv, sib, relay, rs, blk, start, part, parts, mine, left, at, ap, mg, mw,
    load_sem, p1_send, p1_recv, p2_send, p2_recv, p3_sem, p4_sem, p5_sem, p7_send, p7_recv,
    p8_send, p8_recv, p9_send, p9_recv,
):
    chips = replicas // 2
    width = tiles * LANES
    half = blk.shape[1]
    r = lax.axis_index("replica")
    f = lax.axis_index("fsdp")
    c = lax.rem(r, 2)
    y = r // 2
    sibling = {"replica": 2 * y + 1 - c, "fsdp": f}
    shifts = [2, 1, 3, 0]

    def cols(block):
        return pl.ds(pl.multiple_of(block * width, LANES), width)

    def chip(shift):
        return lax.rem(y + shift, chips)

    def along_y(shift):
        return {"replica": 2 * chip(shift) + c, "fsdp": f}

    def send(src, dst, s, d, to):
        pltpu.make_async_remote_copy(
            src_ref=src, dst_ref=dst, send_sem=s, recv_sem=d, device_id=to, device_id_type=MESH
        ).start()

    drains = []

    def finish():
        for condition, ref, sem in drains:
            if condition is None:
                wait_for(ref, sem)
            else:

                @pl.when(condition)
                def _():
                    wait_for(ref, sem)

    order = [2 * chip(s) + 1 - c for s in shifts] + [2 * chip(s) + c for s in shifts]
    loads = []
    for n, block in enumerate(order):
        at_cols = cols(block)
        three = [
            pltpu.make_async_copy(src.at[:, :, at_cols], dst.at[:, :, at_cols], load_sem.at[n, i])
            for i, (src, dst) in enumerate(((lp_hbm, cor), (base_hbm, basev), (err_hbm, errv)))
        ]
        for copy in three:
            copy.start()
        loads.append(three)

    barrier = pltpu.get_barrier_semaphore()
    for k in range(1, replicas):
        pl.semaphore_signal(
            barrier, inc=1, device_id={"replica": lax.rem(r + k, replicas), "fsdp": f}, device_id_type=MESH
        )
    def greet(k, _):
        for core in range(2):
            pl.semaphore_signal(
                barrier, inc=1, device_id={"replica": 2 * y + core, "fsdp": lax.rem(f + k, fsdp)}, device_id_type=MESH
            )
        return 0

    lax.fori_loop(1, fsdp, greet, 0)

    def correct(n):
        for copy in loads[n]:
            copy.wait()
        at_cols = cols(order[n])
        cor[:, :, at_cols] = basev[:, :, at_cols] - cor[:, :, at_cols] + errv[:, :, at_cols]

    correct(0)
    pl.semaphore_wait(barrier, replicas - 1 + 2 * (fsdp - 1))

    for k in range(chips):
        if k > 0:
            correct(k)
        send(cor.at[:, :, cols(order[k])], sib.at[k], p1_send.at[k], p1_recv.at[k], sibling)
        drains.append((None, sib.at[k], p1_send.at[k]))

    def paired(k):
        correct(chips + k)
        wait_for(sib.at[k], p1_recv.at[k])
        sib[k] = sib[k] + cor[:, :, cols(order[chips + k])]

    def hop(n, src, dst, shift):
        send(src, dst, p2_send.at[n], p2_recv.at[n], along_y(shift))
        drains.append((None, src, p2_send.at[n]))

    paired(0)
    hop(0, sib.at[0, 0], relay.at[0], 1)
    hop(1, sib.at[0, 1], relay.at[1], 3)
    paired(1)
    hop(2, sib.at[1, 1], rs.at[0, 1], 1)
    paired(2)
    hop(3, sib.at[2, 0], rs.at[1, 0], 3)
    paired(3)
    wait_for(relay.at[0], p2_recv.at[0])
    relay[0] = relay[0] + sib[1, 0]
    hop(4, relay.at[0], rs.at[0, 0], 1)
    wait_for(relay.at[1], p2_recv.at[1])
    relay[1] = relay[1] + sib[2, 1]
    hop(5, relay.at[1], rs.at[1, 1], 3)
    write_start_factor(seed_ref[0], r * width, start)
    for n, (a, b) in zip((2, 3, 4, 5), ((0, 1), (1, 0), (0, 0), (1, 1)), strict=True):
        wait_for(rs.at[a, b], p2_recv.at[n])
    blk[...] = (sib[3] + rs[0] + rs[1]) * (1.0 / replicas)

    rows = 2 * half
    part[...] = jnp.dot(
        blk[...].reshape(rows, width), start[...], precision=HIGHEST, preferred_element_type=jnp.float32
    ).reshape(part.shape)
    parts[r] = part[c]
    for k in range(1, replicas):
        to = lax.rem(r + k, replicas)
        send(part.at[lax.rem(to, 2)], parts.at[r], p3_sem.at[0], p3_sem.at[1], {"replica": to, "fsdp": f})
    drains.append((None, parts.at[pl.ds(0, replicas - 1)], p3_sem.at[0]))

    has_tile, my_tile = tile_of(f, 2 * tiles, fsdp)
    owner = jnp.logical_and(has_tile, lax.rem(my_tile, 2) == c)
    other = jnp.logical_not(owner)
    my_tile = my_tile // 2
    for t in range(tiles):
        to = owner_of(2 * t + c, 2 * tiles, fsdp)
        tile = blk.at[:, :, t * LANES : (t + 1) * LANES]

        @pl.when(to != f)
        def _():
            send(tile, at.at[:, f], p5_sem.at[0], p5_sem.at[1], {"replica": r, "fsdp": to})

        @pl.when(to == f)
        def _():
            at[:, f] = tile[...]

    drains.append((owner, at.at[:, pl.ds(0, tiles - 1)], p5_sem.at[0]))
    drains.append((other, at.at[:, pl.ds(0, tiles)], p5_sem.at[0]))

    wait_for(parts.at[pl.ds(0, replicas - 1)], p3_sem.at[1])
    total = parts[0]
    for k in range(1, replicas):
        total = total + parts[k]
    mine[...] = total

    def spread(k, _):
        there = lax.rem(f + k, fsdp)
        has, tile = tile_of(there, 2 * tiles, fsdp)
        core = lax.rem(tile, 2)

        @pl.when(jnp.logical_and(has, jnp.logical_or(k > 0, core != c)))
        def _():
            send(mine, left.at[c * fsdp + f], p4_sem.at[0], p4_sem.at[1], {"replica": 2 * y + core, "fsdp": there})

        return 0

    lax.fori_loop(0, fsdp, spread, 0)
    drains.append((owner, left.at[pl.ds(0, 2 * tiles - 1)], p4_sem.at[0]))
    drains.append((other, left.at[pl.ds(0, 2 * tiles)], p4_sem.at[0]))

    my_cols = pl.ds(pl.multiple_of((r * tiles + my_tile) * LANES, LANES), LANES)

    @pl.when(owner)
    def _():
        left[c * fsdp + f] = total
        wait_for(at.at[:, pl.ds(0, fsdp - 1)], p5_sem.at[1])
        wait_for(left.at[pl.ds(0, 2 * fsdp - 1)], p4_sem.at[1])
        whole = left[...].reshape(fsdp * rows, RANK)
        against = (((0,), (0,)), ((), ()))
        mg[...] = lax.dot_general(
            whole, whole, against, precision=HIGHEST, preferred_element_type=jnp.float32
        ).reshape(mg.shape)
        mw[...] = lax.dot_general(
            whole, at[...].reshape(fsdp * rows, LANES), against, precision=HIGHEST, preferred_element_type=jnp.float32
        ).reshape(mw.shape)
        solve(mg, mw)
        for h in range(2):
            ap[h] = jnp.dot(
                left[pl.ds(h * fsdp, fsdp)].reshape(fsdp * half, RANK),
                mw[...].reshape(RANK, LANES),
                precision=HIGHEST,
                preferred_element_type=jnp.float32,
            ).reshape(ap.shape[1:])

            def give(k, _):
                to = lax.rem(f + k, fsdp)
                send(ap.at[h, to], apx.at[h, :, my_cols], p7_send.at[h], p7_recv.at[h], {"replica": r, "fsdp": to})
                return 0

            lax.fori_loop(1, fsdp, give, 0)
            apx[h, :, my_cols] = ap[h, f]

    def place(h, block):
        return apx.at[h, :, cols(block)]

    for h in range(2):
        drains.append((owner, ap.at[0, pl.ds(0, fsdp - 1)], p7_send.at[h]))

        @pl.when(owner)
        def _():
            wait_for(ap.at[0, pl.ds(0, tiles - 1)], p7_recv.at[h])

        @pl.when(other)
        def _():
            wait_for(ap.at[0, pl.ds(0, tiles)], p7_recv.at[h])

        for k, shift in enumerate(shifts):
            if shift:
                send(place(h, r), place(h, r), p8_send.at[h, k], p8_recv.at[h, k], along_y(shift))
                drains.append((None, blk.at[0], p8_send.at[h, k]))
            else:
                send(place(h, r), place(h, r), p9_send.at[h, k], p9_recv.at[h, k], sibling)
            drains.append((None, blk.at[0], p9_send.at[h, k]))

    for h in range(2):
        for k in (1, 2, 0):
            block = 2 * chip(chips - shifts[k]) + c
            wait_for(place(h, block), p8_recv.at[h, k])
            send(place(h, block), place(h, block), p9_send.at[h, k], p9_recv.at[h, k], sibling)
    for h in range(2):
        for k in range(chips):
            wait_for(blk.at[0], p9_recv.at[h, k])
    finish()


def approximate(local_params, outer_base, error_memory, start_seed):
    replicas, fsdp = lax.axis_size("replica"), lax.axis_size("fsdp")
    rows, columns = outer_base.shape
    half = rows // 2
    tiles = columns // replicas // LANES
    width = tiles * LANES
    chips = replicas // 2
    f32 = jnp.float32
    whole = (2, half, columns)
    dma = pltpu.SemaphoreType.DMA
    in_hbm = pl.BlockSpec(memory_space=pltpu.HBM)
    found = pl.pallas_call(
        functools.partial(kernel, replicas, fsdp, tiles),
        out_shape=[pltpu.VMEM(whole, f32)] * 3,
        in_specs=[pl.BlockSpec(memory_space=pltpu.SMEM), in_hbm, in_hbm, in_hbm],
        out_specs=[pl.BlockSpec(memory_space=pltpu.VMEM)] * 3,
        scratch_shapes=[
            pltpu.VMEM(whole, f32),
            pltpu.VMEM((chips, 2, half, width), f32),
            pltpu.VMEM((2, half, width), f32),
            pltpu.VMEM((2, 2, half, width), f32),
            pltpu.VMEM((2, half, width), f32),
            pltpu.VMEM((width, RANK), f32),
            pltpu.VMEM((2, half, RANK), f32),
            pltpu.VMEM((replicas, half, RANK), f32),
            pltpu.VMEM((half, RANK), f32),
            pltpu.VMEM((2 * fsdp, half, RANK), f32),
            pltpu.VMEM((2, fsdp, half, LANES), f32),
            pltpu.VMEM((2, fsdp, half, LANES), f32),
            pltpu.VMEM((RANK // SUBS, SUBS, RANK), f32),
            pltpu.VMEM((RANK // SUBS, SUBS, LANES), f32),
            dma((replicas, 3)),
            dma((chips,)),
            dma((chips,)),
            dma((6,)),
            dma((6,)),
            dma((2,)),
            dma((2,)),
            dma((2,)),
            dma((2,)),
            dma((2,)),
            dma((2, chips)),
            dma((2, chips)),
            dma((2, chips)),
            dma((2, chips)),
        ],
        compiler_params=pltpu.CompilerParams(
            collective_id=0, has_side_effects=True, vmem_limit_bytes=61 * 1024 * 1024
        ),
        cost_estimate=pl.CostEstimate(flops=10**9, bytes_accessed=4 * 10**6, transcendentals=0),
        name="approximate",
    )(
        start_seed,
        local_params.reshape(whole),
        outer_base.reshape(whole),
        error_memory.reshape(whole),
    )
    return [x.reshape(rows, columns) for x in found]


def on_device(local_params, outer_base, error_memory, momentum, start_seed):
    approx, corrected, base = approximate(local_params[0], outer_base, error_memory[0], start_seed)
    new_error = (corrected - approx)[None]
    new_momentum = 0.9 * momentum + approx
    new_base = base - 0.7 * (approx + 0.9 * new_momentum)
    return (new_error, new_base, new_momentum)


def solution(mesh):
    placed = (
        P("replica", "fsdp", None),
        P("fsdp", None),
        P("replica", "fsdp", None),
        P("fsdp", None),
        P(),
    )
    return jax.shard_map(
        on_device,
        mesh=mesh,
        in_specs=placed,
        out_specs=(P("replica", "fsdp", None), P("fsdp", None), P("fsdp", None)),
        check_vma=False,
    )
```

time: 62.2 us -> 56.7 us (0.912)
  Pallas kernels: 55.4 us -> 52.3 us
  local copies, waits for them, and re-layouts: 3.53 us -> 0.49 us
  other arithmetic: 1.75 us -> 2.46 us
    pallas_call x1, Pallas kernels: 55.4 us -> 52.3 us  [approximate(): pl.pallas_call(functools.partial(kernel, replicas, fsdp, tiles), out_shap...]
    unnamed x8 -> x2, local copies, waits for them, and re-layouts: 3.53 us -> 0.49 us
    sub x1 -> x2, other arithmetic: 1.75 us -> 2.46 us  [the longest x1 1.44 us: on_device(): new_base = base - 0.7 * (approx + 0.9 * new_momentum)]
where the time goes in v2:
time: 56.7 us; the launch traced here: 56.5 us
  Pallas kernels  52.3 us (92%)
  other arithmetic  2.46 us (4%)
  between operations  1.29 us (2%)
    pallas_call x1, Pallas kernels, approximate(): pl.pallas_call(functools.partial(kernel, replicas, fsdp, tiles), out_shap...  52.3 us
    sub x1, other arithmetic, on_device(): new_base = base - 0.7 * (approx + 0.9 * new_momentum)  1.44 us

profile of v2, /device:TPU:1, one launch (start us, length us, event | category | flops | bytes accessed | tf_op | source)
XLA Modules:
  0.0 56.5 jit_solution(10560896643892996235)
XLA Ops:
  1.3 52.3 %approximate.1 = (f32[2,8,14336]{2,1,0:T(8,128)S(1)}, f32[2,8,14336]{2,1,0:T(8,128)S(1)}, f32[2,8,14336]{2,1,0:T(8,128)S(1)}) custom-call(s32[1]{0:T(128)S(6)} %copy.8.seed_ref, f32[2,8,14336]{2,1,0:T(8,128)} %bitcast.15, f32[2,8,14336]{2,1,0:T(8,128)} %bitcast.16, f32[2,8,14336]{2,1,0:T(8,128)} %bitcast.17), custom_call_target="tpu_custom_call" | custom-call | flops 1000000000 | bytes 4000000 | tf_op jit(solution)/shard_map/approximate/pallas_call | solution.py:337
  53.6 0.0 copy-start
  53.6 1.0 %subtract_bitcast_fusion = f32[1,16,14336]{2,1,0:T(8,128)} fusion(f32[2,8,14336]{2,1,0:T(8,128)S(1)} %get-tuple-element.6, f32[2,8,14336]{2,1,0:T(8,128)S(1)} %get-tuple-element.7), kind=kLoop, calls=%fused_computation.4 | loop fusion | flops 229376 | bytes 2752512 | tf_op jit(solution)/shard_map/sub | solution.py:388
  54.6 0.5 copy-done
  55.1 1.4 %fusion.1 = (f32[16,14336]{1,0:T(8,128)}, f32[16,14336]{1,0:T(8,128)}) fusion(f32[2,8,14336]{2,1,0:T(8,128)S(1)} %get-tuple-element.7, f32[2,8,14336]{2,1,0:T(8,128)S(1)} %get-tuple-element.8, f32[16,14336]{1,0:T(8,128)S(1)} %copy-done), kind=kLoop, calls=%fused_computation.3 | loop fusion | flops 1376256 | bytes 4587520 | tf_op jit(solution)/shard_map/sub | solution.py:390
Async XLA Ops:
  53.6 1.5 %copy-start = (f32[16,14336]{1,0:T(8,128)S(1)}, f32[16,14336]{1,0:T(8,128)}, u32[]{:S(2)}) copy-start(f32[16,14336]{1,0:T(8,128)} %param.8) | copy-start | bytes 2752516

commit v3 on v2

v3 whole, which is shorter than its diff:
```python
import functools

import jax
import jax.numpy as jnp
from jax import lax
from jax.experimental import pallas as pl
from jax.experimental.pallas import tpu as pltpu
from jax.sharding import PartitionSpec as P

RANK = 128
LANES = 128
SUBS = 8
HIGHEST = lax.Precision.HIGHEST
MESH = pl.DeviceIdType.MESH


def owner_of(tile, tiles, fsdp):
    return tile if tiles == fsdp else tile + 1 + tile // 8


def tile_of(f, tiles, fsdp):
    if tiles == fsdp:
        return f >= 0, f
    tile = f - 1 - f // 9
    return jnp.logical_and(lax.rem(f, 9) != 0, tile < tiles), tile


def write_start_factor(seed, first_row, out_ref):
    two = 2 * SUBS
    k = lax.broadcasted_iota(jnp.int32, (two, LANES), 1)
    j = lax.broadcasted_iota(jnp.int32, (two, LANES), 0) + first_row
    mixed = lax.rem(181 * j + 359 * k + 1013 * seed, 65521)
    added = 7 * j + 3 * k

    def rows(i, carry):
        mixed, added = carry
        low = jnp.where(mixed >= 65498, mixed - 65498, jnp.where(mixed >= 32749, mixed - 32749, mixed))
        value = mixed * low + added
        quotient = (value.astype(jnp.float32) * ((1.0 - 2.0**-21) / 65521.0)).astype(jnp.int32)
        rest = value - quotient * 65521
        rest = jnp.where(rest >= 65521, rest - 65521, rest)
        odd = 2 * rest - 65521
        high = (odd + 256) >> 9
        here = pl.ds(pl.multiple_of(i * two, two), two)
        out_ref[here, :LANES] = high.astype(jnp.float32).astype(jnp.bfloat16)
        out_ref[here, LANES:] = (odd - 512 * high).astype(jnp.float32).astype(jnp.bfloat16)
        mixed = mixed + 181 * two
        return jnp.where(mixed >= 65521, mixed - 65521, mixed), added + 7 * two

    lax.fori_loop(0, out_ref.shape[0] // two, rows, (mixed, added), unroll=8)


def times_start_factor(x, start):
    parts, rest = [], x
    for _ in range(3):
        parts.append(rest.astype(jnp.bfloat16))
        rest = rest - parts[-1].astype(jnp.float32)
    both = jnp.dot(jnp.concatenate(parts, axis=0), start, preferred_element_type=jnp.float32)
    wide = 512.0 * both[:, :LANES] + both[:, LANES:]
    n = x.shape[0]
    return (wide[2 * n :] + wide[n : 2 * n]) + wide[:n]


def invert(m):
    sub = lax.broadcasted_iota(jnp.int32, (SUBS, LANES), 0)
    lane = lax.broadcasted_iota(jnp.int32, (SUBS, LANES), 1)

    def col(x, at):
        return jnp.broadcast_to(x[:, at : at + 1], (SUBS, LANES))

    def row(x, i):
        return jnp.broadcast_to(x[i : i + 1, :], (SUBS, LANES))

    panels = RANK // SUBS
    for p in range(panels):
        first = SUBS * p
        x = m[p]
        cols = [col(x, first + j) for j in range(SUBS)]
        inside = jnp.logical_and(lane >= first, lane < first + SUBS)
        x = jnp.where(inside, jnp.where(lane - first == sub, 1.0, 0.0), x)
        for i in range(SUBS):
            scale = 1.0 / row(cols[i], i)
            here = sub == i
            by = cols[i]

            def step(x):
                pivot_row = row(x, i) * scale
                return jnp.where(here, pivot_row, x - by * pivot_row)

            x = step(x)
            for j in range(i + 1, SUBS):
                cols[j] = step(cols[j])
        rows = [row(x, j) for j in range(SUBS)]
        for q in [(p + 1 + k) % panels for k in range(panels - 1)]:
            a = m[q]
            t = [col(a, first + j) * rows[j] for j in range(SUBS)]
            taken = ((t[0] + t[1]) + (t[2] + t[3])) + ((t[4] + t[5]) + (t[6] + t[7]))
            m[q] = jnp.where(inside, 0.0, a) - taken
        m[p] = x


def along_x(fsdp):
    return 4 if fsdp % 8 == 0 else 2


def wait_for(ref, sem):
    if 0 in ref.shape:
        return
    pltpu.make_async_copy(ref, ref, sem).wait()


def kernel(
    replicas, fsdp, tiles,
    seed_ref, lp_hbm, base_hbm, err_hbm, mom_hbm, cor, basev, momv,
    errv, sib, relay, rs, blk, start, part, parts, line, left, at, ap, apx, mg,
    load_sem, mom_sem, p1_send, p1_recv, p2_send, p2_recv, p3_sem, pz_sem, px_send, px_recv, p5_sem, p7_send, p7_recv,
    p8_send, p8_recv, p9_send, p9_recv,
):
    chips = replicas // 2
    width = tiles * LANES
    half = blk.shape[2]
    rows = 2 * half
    r = lax.axis_index("replica")
    f = lax.axis_index("fsdp")
    c = lax.rem(r, 2)
    y = r // 2
    nx = along_x(fsdp)
    nz = fsdp // nx
    z, x = f // nx, lax.rem(f, nx)
    sibling = {"replica": 2 * y + 1 - c, "fsdp": f}
    shifts = [2, 1, 3, 0]

    def cols(block):
        return pl.ds(pl.multiple_of(block * width, LANES), width)

    def chip(shift):
        return lax.rem(y + shift, chips)

    def along_y(shift):
        return {"replica": 2 * chip(shift) + c, "fsdp": f}

    def send(src, dst, s, d, to):
        pltpu.make_async_remote_copy(
            src_ref=src, dst_ref=dst, send_sem=s, recv_sem=d, device_id=to, device_id_type=MESH
        ).start()

    drains = []

    def finish():
        for condition, ref, sem in drains:
            if condition is None:
                wait_for(ref, sem)
            else:

                @pl.when(condition)
                def _():
                    wait_for(ref, sem)

    def in_line(f):
        return lax.rem(f, nx) * nz + f // nx

    order = [2 * chip(s) + 1 - c for s in shifts] + [2 * chip(s) + c for s in shifts]
    loads = []

    def load(k):
        two = pl.ds(pl.multiple_of(chip(shifts[k]) * 2 * width, LANES), 2 * width)
        copies = [
            pltpu.make_async_copy(src.at[:, :, two], dst.at[:, :, two], load_sem.at[k, i])
            for i, (src, dst) in enumerate(((lp_hbm, cor), (base_hbm, basev), (err_hbm, errv)))
        ]
        for copy in copies:
            copy.start()
        loads.append(copies)

    load(0)
    barrier = pltpu.get_barrier_semaphore()

    def greet(replica, there):
        pl.semaphore_signal(barrier, inc=1, device_id={"replica": replica, "fsdp": there}, device_id_type=MESH)

    for k in range(1, replicas):
        greet(lax.rem(r + k, replicas), f)
    for k in range(1, nx):
        greet(2 * y + 1 - c, z * nx + lax.rem(x + k, nx))
    for k in range(1, fsdp):
        greet(r, lax.rem(f + k, fsdp))
    for k in range(1, chips):
        load(k)
    load_momentum = pltpu.make_async_copy(mom_hbm, momv, mom_sem.at[0])

    def correct(n):
        if n < chips:
            for copy in loads[n]:
                copy.wait()
        at_cols = cols(order[n])
        cor[:, :, at_cols] = basev[:, :, at_cols] - cor[:, :, at_cols] + errv[:, :, at_cols]

    for k in range(chips):
        write_start_factor(seed_ref[0], order[chips + k] * width, start.at[k])
        correct(k)
        if k == 0:
            pl.semaphore_wait(barrier, replicas - 1 + nx - 1 + fsdp - 1)
        send(cor.at[:, :, cols(order[k])], sib.at[k], p1_send.at[k], p1_recv.at[k], sibling)
    load_momentum.start()
    for k in range(chips):
        correct(chips + k)

    def paired(k):
        wait_for(sib.at[k], p1_recv.at[k])
        sib[k] = sib[k] + cor[:, :, cols(order[chips + k])]

    def hop(n, src, dst, shift):
        send(src, dst, p2_send.at[n], p2_recv.at[n], along_y(shift))
        drains.append((None, src, p2_send.at[n]))

    paired(0)
    hop(0, sib.at[0, 0], relay.at[0], 1)
    hop(1, sib.at[0, 1], relay.at[1], 3)

    scale = 3.4641016 / 65521.0 / 2.0 / replicas
    left_terms = times_start_factor(sib[0].reshape(rows, width), start[0])
    for k in range(1, chips):
        paired(k)
        left_terms = left_terms + times_start_factor(sib[k].reshape(rows, width), start[k])
    part[...] = (left_terms * scale).reshape(part.shape)
    parts[r] = part[c]
    for k in range(1, replicas):
        to = lax.rem(r + k, replicas)
        send(part.at[lax.rem(to, 2)], parts.at[r], p3_sem.at[0], p3_sem.at[1], {"replica": to, "fsdp": f})
    drains.append((None, parts.at[pl.ds(0, replicas - 1)], p3_sem.at[0]))

    hop(2, sib.at[1, 1], rs.at[0, 1], 1)
    hop(3, sib.at[2, 0], rs.at[1, 0], 3)
    wait_for(relay.at[0], p2_recv.at[0])
    relay[0] = relay[0] + sib[1, 0]
    hop(4, relay.at[0], rs.at[0, 0], 1)
    wait_for(relay.at[1], p2_recv.at[1])
    relay[1] = relay[1] + sib[2, 1]
    hop(5, relay.at[1], rs.at[1, 1], 3)

    wait_for(parts.at[pl.ds(0, replicas - 1)], p3_sem.at[1])
    total = parts[0]
    for k in range(1, replicas):
        total = total + parts[k]
    line[z] = total

    has_tile, my_tile = tile_of(f, 2 * tiles, fsdp)
    owner = jnp.logical_and(has_tile, lax.rem(my_tile, 2) == c)
    other = jnp.logical_not(owner)
    my_tile = my_tile // 2

    def to_owner(t):
        to = owner_of(2 * t + c, 2 * tiles, fsdp)
        tile = blk.at[t]

        @pl.when(to != f)
        def _():
            send(tile, at.at[in_line(f)], p5_sem.at[0], p5_sem.at[1], {"replica": r, "fsdp": to})

        @pl.when(to == f)
        def _():
            at[in_line(f)] = tile[...]

    for k in range(1, nz):
        to = lax.rem(z + k, nz) * nx + x
        send(line.at[z], line.at[z], pz_sem.at[0], pz_sem.at[1], {"replica": r, "fsdp": to})
    drains.append((None, line.at[pl.ds(0, nz - 1)], pz_sem.at[0]))
    wait_for(line.at[pl.ds(0, nz - 1)], pz_sem.at[1])
    for k in range(nx):
        there = z * nx + lax.rem(x + k, nx)
        has, tile = tile_of(there, 2 * tiles, fsdp)
        core = lax.rem(tile, 2)
        remote = has if k else jnp.logical_and(has, core != c)

        @pl.when(remote)
        def _():
            send(line, left.at[c * nx + x], px_send.at[k], px_recv.at[0], {"replica": 2 * y + core, "fsdp": there})

        drains.append((remote, line, px_send.at[k]))
    for n, (a, b) in zip((2, 3, 4, 5), ((0, 1), (1, 0), (0, 0), (1, 1)), strict=True):
        wait_for(rs.at[a, b], p2_recv.at[n])
    mean = (sib[3] + rs[0] + rs[1]) * (1.0 / replicas)
    for t in range(tiles):
        blk[t] = mean[:, :, t * LANES : (t + 1) * LANES]
    for t in range(tiles):
        to_owner(t)
    drains.append((owner, at.at[pl.ds(0, tiles - 1)], p5_sem.at[0]))
    drains.append((other, at.at[pl.ds(0, tiles)], p5_sem.at[0]))

    cut = tiles // 2
    sizes = (cut, tiles - cut)
    my_half = my_tile // cut
    my_tile = r * tiles + my_tile

    @pl.when(owner)
    def _():
        left[c * nx + x] = line[...]
        wait_for(left.at[pl.ds(0, 2 * nx - 1)], px_recv.at[0])
        whole = left[...].reshape(fsdp * rows, RANK)
        against = (((0,), (0,)), ((), ()))
        mg[...] = lax.dot_general(
            whole, whole, against, precision=HIGHEST, preferred_element_type=jnp.float32
        ).reshape(mg.shape)
        invert(mg)
        wait_for(at.at[pl.ds(0, fsdp - 1)], p5_sem.at[1])

        def left_half(h):
            return left[pl.ds(h * nx, nx)].reshape(fsdp * half, RANK)

        products = [
            lax.dot_general(
                left_half(h),
                at[:, h].reshape(fsdp * half, LANES),
                against,
                precision=HIGHEST,
                preferred_element_type=jnp.float32,
            )
            for h in range(2)
        ]
        weights = jnp.dot(
            mg[...].reshape(RANK, RANK),
            products[0] + products[1],
            precision=HIGHEST,
            preferred_element_type=jnp.float32,
        )
        for h in range(2):
            ap[:, h] = jnp.dot(
                left_half(h), weights, precision=HIGHEST, preferred_element_type=jnp.float32
            ).reshape(fsdp, half, LANES)

        def give(k, _):
            to = lax.rem(f + k, fsdp)
            send(ap.at[in_line(to)], apx.at[my_tile], p7_send.at[0], p7_recv.at[my_half], {"replica": r, "fsdp": to})
            return 0

        lax.fori_loop(1, fsdp, give, 0)
        apx[my_tile] = ap[in_line(f)]

    def returned(h):
        mine_too = jnp.logical_and(owner, my_half == h)

        @pl.when(mine_too)
        def _():
            wait_for(apx.at[pl.ds(0, sizes[h] - 1)], p7_recv.at[h])

        @pl.when(jnp.logical_not(mine_too))
        def _():
            wait_for(apx.at[pl.ds(0, sizes[h])], p7_recv.at[h])

    drains.append((owner, ap.at[pl.ds(0, fsdp - 1)], p7_send.at[0]))
    def place(block, h):
        return apx.at[pl.ds(block * tiles + h * cut, sizes[h])]

    def end(block, h):
        for t in range(sizes[h]):
            tile = block * tiles + h * cut + t
            at_cols = pl.ds(pl.multiple_of(tile * LANES, LANES), LANES)
            found = apx[tile]
            cor[:, :, at_cols] = cor[:, :, at_cols] - found
            momentum = 0.9 * momv[:, :, at_cols] + found
            momv[:, :, at_cols] = momentum
            basev[:, :, at_cols] = basev[:, :, at_cols] - 0.7 * (found + 0.9 * momentum)

    def pass_on(h):
        for k, shift in enumerate(shifts[:-1]):
            send(place(r, h), place(r, h), p8_send.at[h, k], p8_recv.at[h, k], along_y(shift))
            drains.append((None, place(r, h), p8_send.at[h, k]))
        send(place(r, h), place(r, h), p9_send.at[h, chips - 1], p9_recv.at[h, chips - 1], sibling)
        drains.append((None, place(r, h), p9_send.at[h, chips - 1]))

    returned(0)
    pass_on(0)
    load_momentum.wait()
    for k in range(chips):
        wait_for(sib.at[k], p1_send.at[k])
    end(r, 0)
    returned(1)
    pass_on(1)
    end(r, 1)
    for h in range(2):
        for k in (1, 2, 0):
            block = 2 * chip(chips - shifts[k]) + c
            wait_for(place(block, h), p8_recv.at[h, k])
            send(place(block, h), place(block, h), p9_send.at[h, k], p9_recv.at[h, k], sibling)
            drains.append((None, place(block, h), p9_send.at[h, k]))
            end(block, h)
        for k in (3, 1, 2, 0):
            block = 2 * chip(chips - shifts[k]) + 1 - c
            wait_for(place(block, h), p9_recv.at[h, k])
            end(block, h)
    finish()


def on_device(local_params, outer_base, error_memory, momentum, start_seed):
    replicas, fsdp = lax.axis_size("replica"), lax.axis_size("fsdp")
    rows, columns = outer_base.shape
    half = rows // 2
    tiles = columns // replicas // LANES
    width = tiles * LANES
    chips = replicas // 2
    f32 = jnp.float32
    whole = (2, half, columns)
    dma = pltpu.SemaphoreType.DMA
    in_hbm = pl.BlockSpec(memory_space=pltpu.HBM)
    new_error, new_base, new_momentum = pl.pallas_call(
        functools.partial(kernel, replicas, fsdp, tiles),
        out_shape=[pltpu.VMEM(whole, f32)] * 3,
        in_specs=[pl.BlockSpec(memory_space=pltpu.SMEM), in_hbm, in_hbm, in_hbm, in_hbm],
        out_specs=[pl.BlockSpec(memory_space=pltpu.VMEM)] * 3,
        scratch_shapes=[
            pltpu.VMEM(whole, f32),
            pltpu.VMEM((chips, 2, half, width), f32),
            pltpu.VMEM((2, half, width), f32),
            pltpu.VMEM((2, 2, half, width), f32),
            pltpu.VMEM((tiles, 2, half, LANES), f32),
            pltpu.VMEM((chips, width, 2 * RANK), jnp.bfloat16),
            pltpu.VMEM((2, half, RANK), f32),
            pltpu.VMEM((replicas, half, RANK), f32),
            pltpu.VMEM((fsdp // along_x(fsdp), half, RANK), f32),
            pltpu.VMEM((2 * along_x(fsdp), fsdp // along_x(fsdp), half, RANK), f32),
            pltpu.VMEM((fsdp, 2, half, LANES), f32),
            pltpu.VMEM((fsdp, 2, half, LANES), f32),
            pltpu.VMEM((columns // LANES, 2, half, LANES), f32),
            pltpu.VMEM((RANK // SUBS, SUBS, RANK), f32),
            dma((chips, 3)),
            dma((1,)),
            dma((chips,)),
            dma((chips,)),
            dma((6,)),
            dma((6,)),
            dma((2,)),
            dma((2,)),
            dma((4,)),
            dma((1,)),
            dma((2,)),
            dma((1,)),
            dma((2,)),
            dma((2, chips)),
            dma((2, chips)),
            dma((2, chips)),
            dma((2, chips)),
        ],
        compiler_params=pltpu.CompilerParams(
            collective_id=0, has_side_effects=True, vmem_limit_bytes=60 * 1024 * 1024
        ),
        cost_estimate=pl.CostEstimate(flops=10**9, bytes_accessed=4 * 10**6, transcendentals=0),
        name="approximate",
    )(
        start_seed,
        local_params.reshape(whole),
        outer_base.reshape(whole),
        error_memory.reshape(whole),
        momentum.reshape(whole),
    )
    return (new_error.reshape(1, rows, columns), new_base.reshape(rows, columns), new_momentum.reshape(rows, columns))


def solution(mesh):
    placed = (
        P("replica", "fsdp", None),
        P("fsdp", None),
        P("replica", "fsdp", None),
        P("fsdp", None),
        P(),
    )
    return jax.shard_map(
        on_device,
        mesh=mesh,
        in_specs=placed,
        out_specs=(P("replica", "fsdp", None), P("fsdp", None), P("fsdp", None)),
        check_vma=False,
    )
```

time: 56.7 us -> 53.2 us (0.938)
  Pallas kernels: 52.3 us -> 49 us
  other arithmetic: 2.46 us -> 0 us
  local copies, waits for them, and re-layouts: 0.49 us -> 2.77 us
    pallas_call x1, Pallas kernels: 52.3 us -> 49 us  [on_device(): pl.pallas_call(functools.partial(kernel, replicas, fsdp, tiles), out_shap...]
    sub x2 -> x0, other arithmetic: 2.46 us -> none  [the longest x1 1.44 us: on_device(): new_base = base - 0.7 * (approx + 0.9 * new_momentum)]
    unnamed x2 -> x3, local copies, waits for them, and re-layouts: 0.49 us -> 2.77 us
where the time goes in v3:
time: 53.2 us; the launch traced here: 53.1 us
  Pallas kernels  49 us (92%)
  local copies, waits for them, and re-layouts  2.77 us (5%)
  between operations  1.29 us (2%)
    pallas_call x1, Pallas kernels, on_device(): pl.pallas_call(functools.partial(kernel, replicas, fsdp, tiles), out_shap...  49 us
    unnamed x3, local copies, waits for them, and re-layouts  2.77 us

profile of v3, /device:TPU:1, one launch (start us, length us, event | category | flops | bytes accessed | tf_op | source)
XLA Modules:
  0.0 53.1 jit_solution(4667681907785786104)
XLA Ops:
  1.3 49.0 %approximate.1 = (f32[2,8,14336]{2,1,0:T(8,128)S(1)}, f32[2,8,14336]{2,1,0:T(8,128)S(1)}, f32[2,8,14336]{2,1,0:T(8,128)S(1)}) custom-call(s32[1]{0:T(128)S(6)} %copy.14.seed_ref, f32[2,8,14336]{2,1,0:T(8,128)} %bitcast.10, f32[2,8,14336]{2,1,0:T(8,128)} %bitcast.11, f32[2,8,14336]{2,1,0:T(8,128)} %bitcast.12, f32[2,8,14336]{2,1,0:T(8,128)} %bitcast.13), custom_call_target="tpu_custom_call" | custom-call | flops 1000000000 | bytes 4000000 | tf_op jit(solution)/shard_map/approximate/pallas_call | solution.py:405
  50.3 0.9 %copy.11 = f32[1,16,14336]{2,1,0:T(8,128)} copy(f32[1,16,14336]{2,1,0:T(8,128)S(1)} %bitcast.9) | data formatting | bytes 1835008
  51.2 0.9 %copy.12 = f32[16,14336]{1,0:T(8,128)} copy(f32[16,14336]{1,0:T(8,128)S(1)} %bitcast.8) | data formatting | bytes 1835008
  52.1 0.9 %copy.13 = f32[16,14336]{1,0:T(8,128)} copy(f32[16,14336]{1,0:T(8,128)S(1)} %bitcast.7) | data formatting | bytes 1835008

commit v4 on v3

--- a/solution.py
+++ b/solution.py
@@ -111,7 +111,7 @@
 
 def kernel(
     replicas, fsdp, tiles,
-    seed_ref, lp_hbm, base_hbm, err_hbm, mom_hbm, cor, basev, momv,
+    seed_ref, lp_hbm, base_hbm, err_hbm, mom_hbm, cor, basev, momv, out,
     errv, sib, relay, rs, blk, start, part, parts, line, left, at, ap, apx, mg,
     load_sem, mom_sem, p1_send, p1_recv, p2_send, p2_recv, p3_sem, pz_sem, px_send, px_recv, p5_sem, p7_send, p7_recv,
     p8_send, p8_recv, p9_send, p9_recv,
@@ -127,6 +127,12 @@
     nx = along_x(fsdp)
     nz = fsdp // nx
     z, x = f // nx, lax.rem(f, nx)
+    far_first = [
+        (dz, dx)
+        for dz in sorted(range(nz), key=lambda k: -min(k, nz - k))
+        for dx in range(nx)
+        if dz or dx
+    ]
     sibling = {"replica": 2 * y + 1 - c, "fsdp": f}
     shifts = [2, 1, 3, 0]
 
@@ -221,16 +227,18 @@
     left_terms = times_start_factor(sib[0].reshape(rows, width), start[0])
     for k in range(1, chips):
         paired(k)
+        if k == 1:
+            hop(2, sib.at[1, 1], rs.at[0, 1], 1)
+        if k == 2:
+            hop(3, sib.at[2, 0], rs.at[1, 0], 3)
         left_terms = left_terms + times_start_factor(sib[k].reshape(rows, width), start[k])
     part[...] = (left_terms * scale).reshape(part.shape)
     parts[r] = part[c]
-    for k in range(1, replicas):
+    for k in sorted(range(1, replicas), key=lambda k: -min(k, replicas - k)):
         to = lax.rem(r + k, replicas)
         send(part.at[lax.rem(to, 2)], parts.at[r], p3_sem.at[0], p3_sem.at[1], {"replica": to, "fsdp": f})
     drains.append((None, parts.at[pl.ds(0, replicas - 1)], p3_sem.at[0]))
 
-    hop(2, sib.at[1, 1], rs.at[0, 1], 1)
-    hop(3, sib.at[2, 0], rs.at[1, 0], 3)
     wait_for(relay.at[0], p2_recv.at[0])
     relay[0] = relay[0] + sib[1, 0]
     hop(4, relay.at[0], rs.at[0, 0], 1)
@@ -261,29 +269,29 @@
         def _():
             at[in_line(f)] = tile[...]
 
-    for k in range(1, nz):
+    for k in sorted(range(1, nz), key=lambda k: -min(k, nz - k)):
         to = lax.rem(z + k, nz) * nx + x
         send(line.at[z], line.at[z], pz_sem.at[0], pz_sem.at[1], {"replica": r, "fsdp": to})
     drains.append((None, line.at[pl.ds(0, nz - 1)], pz_sem.at[0]))
-    wait_for(line.at[pl.ds(0, nz - 1)], pz_sem.at[1])
-    for k in range(nx):
-        there = z * nx + lax.rem(x + k, nx)
-        has, tile = tile_of(there, 2 * tiles, fsdp)
-        core = lax.rem(tile, 2)
-        remote = has if k else jnp.logical_and(has, core != c)
-
-        @pl.when(remote)
-        def _():
-            send(line, left.at[c * nx + x], px_send.at[k], px_recv.at[0], {"replica": 2 * y + core, "fsdp": there})
-
-        drains.append((remote, line, px_send.at[k]))
     for n, (a, b) in zip((2, 3, 4, 5), ((0, 1), (1, 0), (0, 0), (1, 1)), strict=True):
         wait_for(rs.at[a, b], p2_recv.at[n])
     mean = (sib[3] + rs[0] + rs[1]) * (1.0 / replicas)
     for t in range(tiles):
         blk[t] = mean[:, :, t * LANES : (t + 1) * LANES]
     for t in range(tiles):
-        to_owner(t)
+        to_owner(lax.rem(t + f * tiles // fsdp, tiles))
+    wait_for(line.at[pl.ds(0, nz - 1)], pz_sem.at[1])
+    for k in sorted(range(nx), key=lambda k: -min(k, nx - k)):
+        there = z * nx + lax.rem(x + k, nx)
+        has, tile = tile_of(there, 2 * tiles, fsdp)
+        core = lax.rem(tile, 2)
+        remote = has if k else jnp.logical_and(has, core != c)
+
+        @pl.when(remote)
+        def _():
+            send(line, left.at[c * nx + x], px_send.at[k], px_recv.at[0], {"replica": 2 * y + core, "fsdp": there})
+
+        drains.append((remote, line, px_send.at[k]))
     drains.append((owner, at.at[pl.ds(0, tiles - 1)], p5_sem.at[0]))
     drains.append((other, at.at[pl.ds(0, tiles)], p5_sem.at[0]))
 
@@ -328,12 +336,13 @@
                 left_half(h), weights, precision=HIGHEST, preferred_element_type=jnp.float32
             ).reshape(fsdp, half, LANES)
 
-        def give(k, _):
-            to = lax.rem(f + k, fsdp)
+        def give(dz, dx):
+            to = lax.rem(z + dz, nz) * nx + lax.rem(x + dx, nx)
             send(ap.at[in_line(to)], apx.at[my_tile], p7_send.at[0], p7_recv.at[my_half], {"replica": r, "fsdp": to})
             return 0
 
-        lax.fori_loop(1, fsdp, give, 0)
+        for dz, dx in far_first:
+            give(dz, dx)
         apx[my_tile] = ap[in_line(f)]
 
     def returned(h):
@@ -355,11 +364,7 @@
         for t in range(sizes[h]):
             tile = block * tiles + h * cut + t
             at_cols = pl.ds(pl.multiple_of(tile * LANES, LANES), LANES)
-            found = apx[tile]
-            cor[:, :, at_cols] = cor[:, :, at_cols] - found
-            momentum = 0.9 * momv[:, :, at_cols] + found
-            momv[:, :, at_cols] = momentum
-            basev[:, :, at_cols] = basev[:, :, at_cols] - 0.7 * (found + 0.9 * momentum)
+            out[:, :, at_cols] = apx[tile]
 
     def pass_on(h):
         for k, shift in enumerate(shifts[:-1]):
@@ -402,11 +407,11 @@
     whole = (2, half, columns)
     dma = pltpu.SemaphoreType.DMA
     in_hbm = pl.BlockSpec(memory_space=pltpu.HBM)
-    new_error, new_base, new_momentum = pl.pallas_call(
+    corrected, base, old_momentum, approx = pl.pallas_call(
         functools.partial(kernel, replicas, fsdp, tiles),
-        out_shape=[pltpu.VMEM(whole, f32)] * 3,
+        out_shape=[pltpu.VMEM(whole, f32)] * 4,
         in_specs=[pl.BlockSpec(memory_space=pltpu.SMEM), in_hbm, in_hbm, in_hbm, in_hbm],
-        out_specs=[pl.BlockSpec(memory_space=pltpu.VMEM)] * 3,
+        out_specs=[pl.BlockSpec(memory_space=pltpu.VMEM)] * 4,
         scratch_shapes=[
             pltpu.VMEM(whole, f32),
             pltpu.VMEM((chips, 2, half, width), f32),
@@ -441,7 +446,7 @@
             dma((2, chips)),
         ],
         compiler_params=pltpu.CompilerParams(
-            collective_id=0, has_side_effects=True, vmem_limit_bytes=60 * 1024 * 1024
+            collective_id=0, has_side_effects=True, vmem_limit_bytes=59 * 1024 * 1024
         ),
         cost_estimate=pl.CostEstimate(flops=10**9, bytes_accessed=4 * 10**6, transcendentals=0),
         name="approximate",
@@ -452,6 +457,9 @@
         error_memory.reshape(whole),
         momentum.reshape(whole),
     )
+    new_error = corrected - approx
+    new_momentum = 0.9 * old_momentum + approx
+    new_base = base - 0.7 * (approx + 0.9 * new_momentum)
     return (new_error.reshape(1, rows, columns), new_base.reshape(rows, columns), new_momentum.reshape(rows, columns))
 
 

time: 53.2 us -> 51 us (0.959)
  local copies, waits for them, and re-layouts: 2.77 us -> 0 us
  other arithmetic: 0 us -> 1.76 us
  Pallas kernels: 49 us -> 47.9 us
    unnamed x3 -> x0, local copies, waits for them, and re-layouts: 2.77 us -> none
    reshape x0 -> x1, other arithmetic: none -> 1.76 us  [on_device(): new_momentum.reshape(rows, columns)]
    pallas_call x1, Pallas kernels: 49 us -> 47.9 us  [on_device(): pl.pallas_call(functools.partial(kernel, replicas, fsdp, tiles), out_shap...]
where the time goes in v4:
time: 51 us; the launch traced here: 50.9 us
  Pallas kernels  47.9 us (94%)
  other arithmetic  1.76 us (3%)
  between operations  1.29 us (3%)
    pallas_call x1, Pallas kernels, on_device(): pl.pallas_call(functools.partial(kernel, replicas, fsdp, tiles), out_shap...  47.9 us
    reshape x1, other arithmetic, on_device(): new_momentum.reshape(rows, columns)  1.76 us

profile of v4, /device:TPU:1, one launch (start us, length us, event | category | flops | bytes accessed | tf_op | source)
XLA Modules:
  0.0 50.9 jit_solution(17116147853577273998)
XLA Ops:
  1.3 47.9 %approximate.1 = (f32[2,8,14336]{2,1,0:T(8,128)S(1)}, f32[2,8,14336]{2,1,0:T(8,128)S(1)}, f32[2,8,14336]{2,1,0:T(8,128)S(1)}, f32[2,8,14336]{2,1,0:T(8,128)S(1)}) custom-call(s32[1]{0:T(128)S(6)} %copy.8.seed_ref, f32[2,8,14336]{2,1,0:T(8,128)} %bitcast.10, f32[2,8,14336]{2,1,0:T(8,128)} %bitcast.11, f32[2,8,14336]{2,1,0:T(8,128)} %bitcast.12, ...), custom_call_target="tpu_custom_call" | custom-call | flops 1000000000 | bytes 4000000 | tf_op jit(solution)/shard_map/approximate/pallas_call | solution.py:410
  49.2 1.8 %fusion = (f32[16,14336]{1,0:T(8,128)}, f32[16,14336]{1,0:T(8,128)}, f32[1,16,14336]{2,1,0:T(8,128)}) fusion(f32[2,8,14336]{2,1,0:T(8,128)S(1)} %get-tuple-element.8, f32[2,8,14336]{2,1,0:T(8,128)S(1)} %get-tuple-element.10, f32[2,8,14336]{2,1,0:T(8,128)S(1)} %get-tuple-element.9, f32[2,8,14336]{2,1,0:T(8,128)S(1)} %get-tuple-element.7), kind=kLoop, calls=%fused_computation.3 | loop fusion | flops 1605632 | bytes 6422528 | tf_op jit(solution)/shard_map/reshape | solution.py:463

commit v5 on v4

--- a/solution.py
+++ b/solution.py
@@ -78,18 +78,20 @@
         cols = [col(x, first + j) for j in range(SUBS)]
         inside = jnp.logical_and(lane >= first, lane < first + SUBS)
         x = jnp.where(inside, jnp.where(lane - first == sub, 1.0, 0.0), x)
+        scales = jnp.ones_like(x)
         for i in range(SUBS):
-            scale = 1.0 / row(cols[i], i)
-            here = sub == i
-            by = cols[i]
+            pivot = row(cols[i], i)
+            scale = 1.0 / pivot
+            scales = jnp.where(sub == i, scale, scales)
+            by = jnp.where(sub == i, 0.0, cols[i])
 
             def step(x):
-                pivot_row = row(x, i) * scale
-                return jnp.where(here, pivot_row, x - by * pivot_row)
+                return x - by * (row(x, i) * scale)
 
             x = step(x)
             for j in range(i + 1, SUBS):
                 cols[j] = step(cols[j])
+        x = x * scales
         rows = [row(x, j) for j in range(SUBS)]
         for q in [(p + 1 + k) % panels for k in range(panels - 1)]:
             a = m[q]
@@ -130,7 +132,7 @@
     far_first = [
         (dz, dx)
         for dz in sorted(range(nz), key=lambda k: -min(k, nz - k))
-        for dx in range(nx)
+        for dx in sorted(range(nx), key=lambda k: -min(k, nx - k))
         if dz or dx
     ]
     sibling = {"replica": 2 * y + 1 - c, "fsdp": f}

time: 51 us -> 50.7 us (level)
  no operation moved by 1% of the time
where the time goes in v5:
time: 50.7 us
  Pallas kernels  47.6 us (94%)
  other arithmetic  1.76 us (3%)
  between operations  1.29 us (3%)
    pallas_call x1, Pallas kernels, on_device(): pl.pallas_call(functools.partial(kernel, replicas, fsdp, tiles), out_shap...  47.6 us
    reshape x1, other arithmetic, on_device(): new_momentum.reshape(rows, columns)  1.76 us

profile of v5, /device:TPU:1, one launch (start us, length us, event | category | flops | bytes accessed | tf_op | source)
XLA Modules:
  0.0 50.7 jit_solution(12396574092046566589)
XLA Ops:
  1.3 47.6 %approximate.1 = (f32[2,8,14336]{2,1,0:T(8,128)S(1)}, f32[2,8,14336]{2,1,0:T(8,128)S(1)}, f32[2,8,14336]{2,1,0:T(8,128)S(1)}, f32[2,8,14336]{2,1,0:T(8,128)S(1)}) custom-call(s32[1]{0:T(128)S(6)} %copy.8.seed_ref, f32[2,8,14336]{2,1,0:T(8,128)} %bitcast.10, f32[2,8,14336]{2,1,0:T(8,128)} %bitcast.11, f32[2,8,14336]{2,1,0:T(8,128)} %bitcast.12, ...), custom_call_target="tpu_custom_call" | custom-call | flops 1000000000 | bytes 4000000 | tf_op jit(solution)/shard_map/approximate/pallas_call | solution.py:412
  48.9 1.8 %fusion = (f32[16,14336]{1,0:T(8,128)}, f32[16,14336]{1,0:T(8,128)}, f32[1,16,14336]{2,1,0:T(8,128)}) fusion(f32[2,8,14336]{2,1,0:T(8,128)S(1)} %get-tuple-element.8, f32[2,8,14336]{2,1,0:T(8,128)S(1)} %get-tuple-element.10, f32[2,8,14336]{2,1,0:T(8,128)S(1)} %get-tuple-element.9, f32[2,8,14336]{2,1,0:T(8,128)S(1)} %get-tuple-element.7), kind=kLoop, calls=%fused_computation.3 | loop fusion | flops 1605632 | bytes 6422528 | tf_op jit(solution)/shard_map/reshape | solution.py:465

commit v6 on v5

--- a/solution.py
+++ b/solution.py
@@ -180,7 +180,8 @@
             copy.start()
         loads.append(copies)
 
-    load(0)
+    for k in range(chips):
+        load(k)
     barrier = pltpu.get_barrier_semaphore()
 
     def greet(replica, there):
@@ -192,8 +193,6 @@
         greet(2 * y + 1 - c, z * nx + lax.rem(x + k, nx))
     for k in range(1, fsdp):
         greet(r, lax.rem(f + k, fsdp))
-    for k in range(1, chips):
-        load(k)
     load_momentum = pltpu.make_async_copy(mom_hbm, momv, mom_sem.at[0])
 
     def correct(n):

time: 50.7 us -> 50.8 us (level)
  no operation moved by 1% of the time
where the time goes in v6:
time: 50.8 us; the launch traced here: 50.7 us
  Pallas kernels  47.6 us (94%)
  other arithmetic  1.76 us (3%)
  between operations  1.29 us (3%)
    pallas_call x1, Pallas kernels, on_device(): pl.pallas_call(functools.partial(kernel, replicas, fsdp, tiles), out_shap...  47.6 us
    reshape x1, other arithmetic, on_device(): new_momentum.reshape(rows, columns)  1.76 us

profile of v6, /device:TPU:1, one launch (start us, length us, event | category | flops | bytes accessed | tf_op | source)
XLA Modules:
  0.0 50.7 jit_solution(104417727396873400)
XLA Ops:
  1.3 47.6 %approximate.1 = (f32[2,8,14336]{2,1,0:T(8,128)S(1)}, f32[2,8,14336]{2,1,0:T(8,128)S(1)}, f32[2,8,14336]{2,1,0:T(8,128)S(1)}, f32[2,8,14336]{2,1,0:T(8,128)S(1)}) custom-call(s32[1]{0:T(128)S(6)} %copy.8.seed_ref, f32[2,8,14336]{2,1,0:T(8,128)} %bitcast.10, f32[2,8,14336]{2,1,0:T(8,128)} %bitcast.11, f32[2,8,14336]{2,1,0:T(8,128)} %bitcast.12, ...), custom_call_target="tpu_custom_call" | custom-call | flops 1000000000 | bytes 4000000 | tf_op jit(solution)/shard_map/approximate/pallas_call | solution.py:411
  48.9 1.8 %fusion = (f32[16,14336]{1,0:T(8,128)}, f32[16,14336]{1,0:T(8,128)}, f32[1,16,14336]{2,1,0:T(8,128)}) fusion(f32[2,8,14336]{2,1,0:T(8,128)S(1)} %get-tuple-element.8, f32[2,8,14336]{2,1,0:T(8,128)S(1)} %get-tuple-element.10, f32[2,8,14336]{2,1,0:T(8,128)S(1)} %get-tuple-element.9, f32[2,8,14336]{2,1,0:T(8,128)S(1)} %get-tuple-element.7), kind=kLoop, calls=%fused_computation.3 | loop fusion | flops 1605632 | bytes 6422528 | tf_op jit(solution)/shard_map/reshape | solution.py:464
